TPU v7x, 32 devices: a whole 2x2x4 slice. The times are simulated.
32 devices in a mesh: groups: 2 (over x), wide: 8 (over z, y), narrow: 2 (over core).
Axes of the slice: x: 2, y: 2, z: 4, core: 2. Of those that a mesh axis runs over, the one named last changes fastest.
Arguments:
- density: bfloat16 [128, 2, 256, 384], P(('groups', 'wide'), None, 'narrow'), parts along dimension 0, may hold values from -6 to 6
- block_order: int32 [128], P('groups'), parts along dimension 0, may hold values from 0 to 63, as said below
- pattern: int32 [6, 128], P(None, 'groups'), parts along dimension 1, may hold values 0 or 1
- factors: bfloat16 [6, 128, 2, 2, 256, 256], P(None, ('groups', 'wide'), None, None, 'narrow'), parts along dimension 1, may hold values from -0.1875 to 0.1875
- near: bfloat16 [128, 3, 2, 256, 256], P(('groups', 'wide'), None, None, 'narrow'), parts along dimension 0, may hold values from -0.15625 to 0.15625
Outputs:
- potential: float32 [128, 2, 256, 384], P(('groups', 'wide'), None, 'narrow'), parts along dimension 0
There are 2 independent parts, one for each index of `groups`. A program takes and returns all parts, laid end to end along the dimension named above; each array names one. Nothing has to cross between parts.
Inputs may be any that keep to these rules, and one draw needn't show every extreme that they name: `block_order`: a permutation of the blocks; position d * 8 + j (j < 8) holds block (d xor m_j) * 8 + s_j, where the masks m_j (0 .. 7) and the slot permutation s_j depend only on j.
All inputs are finite; a program needn't handle non-finite values.
Results may differ from a plain program's by a relative error of at most 0.0044.
Values may be sent and summed in bfloat16 or wider, within the bound.
A program may use at most 128 MiB of HBM per device.

v0:
```python
import jax
import jax.numpy as jnp
from jax import lax
from jax.sharding import PartitionSpec as P

LEVELS = 6


def swapped(block, axis, distance):
    count = lax.axis_size(axis)
    route = []
    for low in range(count):
        high = low | 1 << distance
        if high != low and high < count:
            route += [(low, high), (high, low)]
    return lax.ppermute(block, axis, route)


def padded_2(cells, sides, width):
    for axis, dim in sides:
        count = lax.axis_size(axis)
        ends = count - 1
        head = lax.slice_in_dim(cells, 0, width, axis=dim)
        tail = lax.slice_in_dim(cells, cells.shape[dim] - width, cells.shape[dim], axis=dim)
        cells = jnp.concatenate(
            [
                lax.ppermute(tail, axis, [(i, (i + 1) % count) for i in range(ends)]),
                cells,
                lax.ppermute(head, axis, [((i + 1) % count, i) for i in range(ends)]),
            ],
            axis=dim,
        )
    return cells


def complex_apply(matrix, vector):
    real_part = jnp.einsum(
        "boi,bir->bor", matrix[:, 0], vector[:, 0], preferred_element_type=jnp.float32
    ) - jnp.einsum("boi,bir->bor", matrix[:, 1], vector[:, 1], preferred_element_type=jnp.float32)
    imag_part = jnp.einsum(
        "boi,bir->bor", matrix[:, 1], vector[:, 0], preferred_element_type=jnp.float32
    ) + jnp.einsum("boi,bir->bor", matrix[:, 0], vector[:, 1], preferred_element_type=jnp.float32)
    return jnp.stack([real_part, imag_part], 1)


def pair_local(vector, bit_pos):
    total = vector.shape[0]
    stride = 1 << bit_pos
    folded = vector.reshape((total // (2 * stride), 2, stride) + vector.shape[1:])
    return folded[:, ::-1].reshape(vector.shape)


def gather_rows(vector):
    return lax.all_gather(vector, "narrow", axis=2, tiled=True)


def per_device(density, block_order, pattern, factors, near):
    blocks_here = density.shape[0]
    wide_at = lax.axis_index("wide")
    wanted = lax.dynamic_slice_in_dim(block_order, wide_at * blocks_here, blocks_here)
    gathered = lax.all_gather(density, "wide", axis=0, tiled=True)
    current = jnp.take(gathered, wanted, axis=0)
    partner_on = lax.dynamic_slice_in_dim(pattern, wide_at * blocks_here, blocks_here, 1).astype(
        jnp.float32
    )
    local_bits = blocks_here.bit_length() - 1
    initial = None
    summed = None
    for level_idx in range(LEVELS):
        full_rows = gather_rows(current)
        if level_idx == 0:
            initial = full_rows
        if level_idx < local_bits:
            partner = pair_local(full_rows, level_idx)
        else:
            partner = swapped(full_rows, "wide", level_idx - local_bits)
        keep = partner_on[level_idx][:, None, None, None]
        summed = complex_apply(factors[level_idx][:, 0], full_rows) + keep * complex_apply(
            factors[level_idx][:, 1], partner
        )
        if level_idx < LEVELS - 1:
            current = summed.astype(jnp.bfloat16)
    padded = padded_2(initial, (("wide", 0),), 1)
    nearby = (
        complex_apply(near[:, 0], padded[:-2])
        + complex_apply(near[:, 1], padded[1:-1])
        + complex_apply(near[:, 2], padded[2:])
    )
    return summed + nearby


def solution(mesh):
    return jax.shard_map(
        per_device,
        mesh=mesh,
        in_specs=(
            P(("groups", "wide"), None, "narrow", None),
            P("groups"),
            P(None, "groups"),
            P(None, ("groups", "wide"), None, None, "narrow", None),
            P(("groups", "wide"), None, None, "narrow", None),
        ),
        out_specs=P(("groups", "wide"), None, "narrow", None),
        check_vma=False,
    )
```

profile of v0, /device:TPU:1, one launch (start us, length us, event | category | flops | bytes accessed | tf_op | source)
XLA Modules:
  0.0 631.7 jit_solution(9425131938120471326)
XLA Ops:
  7.4 180.3 %all-gather.8.cloned.1.call-done = bf16[64,2,128,384]{3,2,1,0:T(8,128)(2,1)} async-done(((bf16[8,2,128,384]{3,2,1,0:T(8,128)(2,1)}), bf16[64,2,128,384]{3,2,1,0:T(8,128)(2,1)}) %all-gather.8.cloned.1.call-update) | async-done | bytes 12582928 | tf_op jit(solution)/shard_map/all_gather | solution.py:61
  187.7 5.5 gather_fusion
  196.3 8.6 %fusion.37 = (bf16[1,8,2,2,128,256]{5,4,3,2,1,0:T(8,128)(2,1)}, bf16[1,8,2,2,128,256]{5,4,3,2,1,0:T(8,128)(2,1)}, bf16[1,8,2,2,128,256]{5,4,3,2,1,0:T(8,128)(2,1...) fusion(bf16[6,8,2,2,128,256]{5,4,3,2,1,0:T(8,128)(2,1)} %param.8), kind=kLoop, calls=%fused_computation.175 | loop fusion | bytes 25165824 | tf_op jit(solution)/shard_map/slice | solution.py:78
  213.8 2.2 add_bitcast_fusion.13
  220.5 3.1 slice_bitcast_fusion.88
  223.6 8.2 %all-gather.12.cloned.1.call-done = bf16[8,2,256,384]{2,3,0,1:T(8,128)(2,1)} async-done(((bf16[8,2,128,384]{2,3,0,1:T(8,128)(2,1)}), bf16[8,2,256,384]{2,3,0,1:T(8,128)(2,1)}) %all-gather.12.cloned.1.call-update) | async-done | bytes 3145744 | tf_op jit(solution)/shard_map/all_gather | solution.py:54
  231.8 3.8 rev.10
  235.6 2.2 fusion.12
  246.9 4.1 copy_bitcast_fusion.2
  252.5 7.0 %all-gather.14.cloned.1.call-done = bf16[8,2,256,384]{2,3,0,1:T(8,128)(2,1)} async-done(((bf16[8,2,128,384]{2,3,0,1:T(8,128)(2,1)}), bf16[8,2,256,384]{2,3,0,1:T(8,128)(2,1)}) %all-gather.14.cloned.1.call-update) | async-done | bytes 3145744 | tf_op jit(solution)/shard_map/all_gather | solution.py:54
  259.5 3.8 rev.11
  263.4 2.2 fusion.16
  274.3 13.0 %all-gather.16.cloned.1.call-done = bf16[8,2,256,384]{2,3,0,1:T(8,128)(2,1)} async-done(((bf16[8,2,128,384]{2,3,0,1:T(8,128)(2,1)}), bf16[8,2,256,384]{2,3,0,1:T(8,128)(2,1)}) %all-gather.16.cloned.1.call-update) | async-done | bytes 3145744 | tf_op jit(solution)/shard_map/all_gather | solution.py:54
  293.6 63.4 %collective-permute-done = bf16[8,2,256,384]{2,3,0,1:T(8,128)(2,1)S(1)} collective-permute-done((bf16[8,2,256,384]{2,3,0,1:T(8,128)(2,1)}, bf16[8,2,256,384]{2,3,0,1:T(8,128)(2,1)S(1)}, u32[]{:S(2)}, u32[]{:S(2)}) %collective-permute-start) | collective-permute-done | bytes 3145760 | tf_op jit(solution)/shard_map/ppermute | solution.py:16
  361.0 13.7 %all-gather.18.cloned.1.call-done = bf16[8,2,256,384]{2,3,0,1:T(8,128)(2,1)} async-done(((bf16[8,2,128,384]{2,3,0,1:T(8,128)(2,1)}), bf16[8,2,256,384]{2,3,0,1:T(8,128)(2,1)}) %all-gather.18.cloned.1.call-update) | async-done | bytes 3145744 | tf_op jit(solution)/shard_map/all_gather | solution.py:54
  376.2 4.0 copy_bitcast_fusion
  384.5 60.0 %collective-permute-done.1 = bf16[8,2,256,384]{2,3,0,1:T(8,128)(2,1)S(1)} collective-permute-done((bf16[8,2,256,384]{2,3,0,1:T(8,128)(2,1)}, bf16[8,2,256,384]{2,3,0,1:T(8,128)(2,1)S(1)}, u32[]{:S(2)}, u32[]{:S(2)}) %collective-permute-start.1) | collective-permute-done | bytes 3145760 | tf_op jit(solution)/shard_map/ppermute | solution.py:16
  448.6 2.2 fusion.38
  454.4 3.3 collective-permute-start.3
  463.9 9.6 %collective-permute-done.3 = bf16[1,2,256,384]{2,3,0,1:T(8,128)(2,1)S(1)} collective-permute-done((bf16[1,2,256,384]{2,3,0,1:T(8,128)(2,1)S(1)}, bf16[1,2,256,384]{2,3,0,1:T(8,128)(2,1)S(1)}, u32[]{:S(2)}, u32[]{:S(2)}) %collective-permute-start.3) | collective-permute-done | bytes 393248 | tf_op jit(solution)/shard_map/ppermute | solution.py:27
  478.8 3.8 collective-permute-start.2
  482.6 2.6 add_bitcast_fusion
  494.3 123.5 %collective-permute-done.2 = bf16[8,2,256,384]{2,3,0,1:T(8,128)(2,1)S(1)} collective-permute-done((bf16[8,2,256,384]{2,3,0,1:T(8,128)(2,1)}, bf16[8,2,256,384]{2,3,0,1:T(8,128)(2,1)S(1)}, u32[]{:S(2)}, u32[]{:S(2)}) %collective-permute-start.2) | collective-permute-done | bytes 3145760 | tf_op jit(solution)/shard_map/ppermute | solution.py:16
  622.3 2.4 copy.37
  (159 shorter events, 85.1 us)
Async XLA Ops:
  6.5 181.2 %all-gather.8.cloned.1.call-start = ((), (), s32[]{:S(2)}) async-start(), calls=%async_computation | async-start | bytes 14155776 | tf_op jit(solution)/shard_map/all_gather | solution.py:61
  7.3 200.8 %all-gather.10.cloned.1.call-start = ((), (), s32[]{:S(2)}) async-start(), calls=%async_computation.1 | async-start | bytes 4718592 | tf_op jit(solution)/shard_map/all_gather | solution.py:54
  195.5 36.3 %all-gather.12.cloned.1.call-start = ((), (), s32[]{:S(2)}) async-start(), calls=%async_computation.2 | async-start | bytes 4718592 | tf_op jit(solution)/shard_map/all_gather | solution.py:54
  210.1 3.1 copy-start.3
  210.1 2.5 copy-start.21
  213.8 2.4 copy-start
  213.8 2.6 copy-start.20
  220.5 39.1 %all-gather.14.cloned.1.call-start = ((), (), s32[]{:S(2)}) async-start(), calls=%async_computation.3 | async-start | bytes 4718592 | tf_op jit(solution)/shard_map/all_gather | solution.py:54
  235.6 2.5 copy-start.4
  246.5 40.8 %all-gather.16.cloned.1.call-start = ((), (), s32[]{:S(2)}) async-start(), calls=%async_computation.4 | async-start | bytes 4718592 | tf_op jit(solution)/shard_map/all_gather | solution.py:54
  263.4 2.5 copy-start.5
  274.3 100.5 %all-gather.18.cloned.1.call-start = ((), (), s32[]{:S(2)}) async-start(), calls=%async_computation.5 | async-start | bytes 4718592 | tf_op jit(solution)/shard_map/all_gather | solution.py:54
  287.3 69.7 %collective-permute-start = (bf16[8,2,256,384]{2,3,0,1:T(8,128)(2,1)}, bf16[8,2,256,384]{2,3,0,1:T(8,128)(2,1)S(1)}, u32[]{:S(2)}, u32[]{:S(2)}) collective-permute-start(bf16[8,2,256,384]{2,3,0,1:T(8,128)(2,1)} %all-gather.16.cloned.1.call-done), channel_id=1, source_target_pairs={{0,2},{2,0},{4,6},{6,4},{8,10},{10,8},{12,14},{14,12},{1,3},{3,1},... | collective-permute-start | bytes 9437192 | tf_op jit(solution)/shard_map/ppermute | solution.py:16
  288.8 2.5 copy-start.12
  361.0 117.9 %all-gather.20.cloned.1.call-start = ((), (), s32[]{:S(2)}) async-start(), calls=%async_computation.6 | async-start | bytes 4718592 | tf_op jit(solution)/shard_map/all_gather | solution.py:54
  374.7 69.8 %collective-permute-start.1 = (bf16[8,2,256,384]{2,3,0,1:T(8,128)(2,1)}, bf16[8,2,256,384]{2,3,0,1:T(8,128)(2,1)S(1)}, u32[]{:S(2)}, u32[]{:S(2)}) collective-permute-start(bf16[8,2,256,384]{2,3,0,1:T(8,128)(2,1)} %all-gather.18.cloned.1.call-done), channel_id=1, source_target_pairs={{0,4},{4,0},{2,6},{6,2},{8,12},{12,8},{10,14},{14,10},{1,5},{5,1},... | collective-permute-start | bytes 9437192 | tf_op jit(solution)/shard_map/ppermute | solution.py:16
  454.4 20.0 %copy-start.16 = (bf16[8,2,128,256]{3,2,0,1:T(8,128)(2,1)}, bf16[8,2,128,256]{3,2,0,1:T(8,128)(2,1)S(1)}, u32[]{:S(2)}) copy-start(bf16[8,2,128,256]{3,2,0,1:T(8,128)(2,1)S(1)} %get-tuple-element.44) | copy-start | bytes 3145732
  454.4 19.1 %collective-permute-start.3 = (bf16[1,2,256,384]{2,3,0,1:T(8,128)(2,1)S(1)}, bf16[1,2,256,384]{2,3,0,1:T(8,128)(2,1)S(1)}, u32[]{:S(2)}, u32[]{:S(2)}) collective-permute-start(bf16[1,2,256,384]{2,3,0,1:T(8,128)(2,1)S(1)} %get-tuple-element.17), channel_id=1, source_target_pairs={{0,2},{2,4},{4,6},{6,8},{8,10},{10,12},{12,14},{1,3},{3,5},{5,7},{... | collective-permute-start | bytes 1179656 | tf_op jit(solution)/shard_map/ppermute | solution.py:27
  457.8 16.5 %collective-permute-start.4 = (bf16[1,2,256,384]{2,3,0,1:T(8,128)(2,1)S(1)}, bf16[1,2,256,384]{2,3,0,1:T(8,128)(2,1)S(1)}, u32[]{:S(2)}, u32[]{:S(2)}) collective-permute-start(bf16[1,2,256,384]{2,3,0,1:T(8,128)(2,1)S(1)} %get-tuple-element.16), channel_id=1, source_target_pairs={{2,0},{4,2},{6,4},{8,6},{10,8},{12,10},{14,12},{3,1},{5,3},{7,5},{... | collective-permute-start | bytes 1179656 | tf_op jit(solution)/shard_map/ppermute | solution.py:29
  474.3 2.8 copy-start.6
  478.8 6.4 %copy-start.7 = (bf16[9,2,256,384]{2,3,0,1:T(8,128)(2,1)S(1)}, bf16[9,2,256,384]{2,3,0,1:T(8,128)(2,1)}, u32[]{:S(2)}) copy-start(bf16[9,2,256,384]{2,3,0,1:T(8,128)(2,1)} %copy-done.6) | copy-start | bytes 10616836
  478.8 6.4 %copy-start.17 = (bf16[8,2,128,256]{3,2,0,1:T(8,128)(2,1)S(1)}, bf16[8,2,128,256]{3,2,0,1:T(8,128)(2,1)}, u32[]{:S(2)}) copy-start(bf16[8,2,128,256]{3,2,0,1:T(8,128)(2,1)} %copy-done.16) | copy-start | bytes 3145732
  478.8 139.0 %collective-permute-start.2 = (bf16[8,2,256,384]{2,3,0,1:T(8,128)(2,1)}, bf16[8,2,256,384]{2,3,0,1:T(8,128)(2,1)S(1)}, u32[]{:S(2)}, u32[]{:S(2)}) collective-permute-start(bf16[8,2,256,384]{2,3,0,1:T(8,128)(2,1)} %all-gather.20.cloned.1.call-done), channel_id=1, source_target_pairs={{0,8},{8,0},{2,10},{10,2},{4,12},{12,4},{6,14},{14,6},{1,9},{9,1},... | collective-permute-start | bytes 9437192 | tf_op jit(solution)/shard_map/ppermute | solution.py:16
  493.7 124.1 %copy-start.14 = (bf16[8,2,128,256]{3,2,0,1:T(8,128)(2,1)S(1)}, bf16[8,2,128,256]{3,2,0,1:T(8,128)(2,1)}, u32[]{:S(2)}) copy-start(bf16[8,2,128,256]{3,2,0,1:T(8,128)(2,1)} %get-tuple-element.20) | copy-start | bytes 3145732
  (17 other events, 30.2 us)
Sparse Core Ops, SparseCore 0:
  9.5 178.0 all-gather.7
  195.6 10.6 all-gather.9
  220.6 11.1 all-gather.11
  246.6 12.8 all-gather.13
  274.4 12.8 all-gather.15
  361.1 13.5 all-gather.17
  448.7 13.5 all-gather.19
where the time goes:
time: 644 us; the launch traced here: 632 us
  waiting for transfers between devices  479 us (74%)
  local copies, waits for them, and re-layouts  66.6 us (10%)
  matrix products  48.7 us (8%)
  between operations  14.3 us (2%)
  starting transfers between devices  12.2 us (2%)
  other arithmetic  10.6 us (2%)
    ppermute x3, waiting for transfers between devices, swapped(): return lax.ppermute(block, axis, route)  247 us
    all_gather x1, waiting for transfers between devices, per_device(): gathered = lax.all_gather(density, 'wide', axis=0, tiled=True)  180 us
    all_gather x6, waiting for transfers between devices, gather_rows(): return lax.all_gather(vector, 'narrow', axis=2, tiled=True)  41.8 us
    unnamed x61, local copies, waits for them, and re-layouts  17.6 us
    dot_general x15, matrix products, complex_apply(): jnp.einsum('boi,bir->bor', matrix[:, 0], vector[:, 0], preferred_element_...  13.4 us
    dot_general x15, matrix products, complex_apply(): jnp.einsum('boi,bir->bor', matrix[:, 1], vector[:, 0], preferred_element_...  12.9 us
  transfers between devices with their start and end apart: 12, of which 9 were waited for; matrix products, arithmetic and copies ran while one was open for 8% of the time, Pallas kernels for 0%

commit v1 on v0

v1 whole, which is shorter than its diff:
```python
import functools

import jax
import jax.numpy as jnp
from jax import lax
from jax.experimental import pallas as pl
from jax.experimental.pallas import tpu as pltpu
from jax.sharding import PartitionSpec as P

LEVELS = 6
LANES = 128
MESH = pl.DeviceIdType.MESH


def flipped(index, distance):
    return index + distance * (1 - 2 * lax.rem(lax.div(index, distance), 2))


def kernel(
    n_wide, x_ref, bits_ref, keep_ref, factors_hbm, near_hbm, out_ref,
    fac, nea, rbuf, xs, full, part, halo, load_sem, send_sem, recv_sem,
):
    chunks, count, rows, lanes = x_ref.shape
    bits = n_wide.bit_length() - 1
    local_bits = count.bit_length() - 1
    me = lax.axis_index("wide")
    core = lax.axis_index("narrow")
    own = pl.ds(pl.multiple_of(core * rows, rows), rows)

    loads = [
        pltpu.make_async_copy(factors_hbm.at[l], fac.at[l], load_sem.at[l]) for l in range(LEVELS)
    ] + [pltpu.make_async_copy(near_hbm, nea, load_sem.at[LEVELS])]
    for load in loads:
        load.start()

    barrier = pltpu.get_barrier_semaphore()
    for other in range(1, n_wide):
        pl.semaphore_signal(
            barrier, inc=1, device_id={"wide": lax.rem(me + other, n_wide)}, device_id_type=MESH
        )
    pl.semaphore_signal(barrier, inc=1, device_id={"narrow": 1 - core}, device_id_type=MESH)
    pl.semaphore_wait(barrier, n_wide)

    made = []
    loaded = set()

    def remote(src, dst, device):
        index = len(made)
        copy = pltpu.make_async_remote_copy(
            src_ref=src, dst_ref=dst, send_sem=send_sem.at[index], recv_sem=recv_sem.at[index],
            device_id=device, device_id_type=MESH,
        )
        made.append(copy)
        return copy

    sibling = {"narrow": 1 - core}
    order = list(range(bits))[::-1]
    route, narrow, wide, forward, rightward, leftward = {}, {}, {}, {}, {}, {}
    for c in range(chunks):
        for i, k in enumerate(order):
            src = x_ref.at[c] if i == 0 else xs.at[i - 1, c]
            route[c, i] = remote(src, rbuf.at[i, c], {"wide": flipped(me, 1 << k)})
        for l in range(LEVELS):
            half = full.at[l, c, :, own, :]
            narrow[c, l] = remote(half, half, sibling)
            if l >= local_bits:
                w = l - local_bits
                held = part.at[w, c, :, own, :]
                wide[c, l] = remote(half, held, {"wide": flipped(me, 1 << w)})
                forward[c, l] = remote(held, held, sibling)
    for c in range(chunks):
        rightward[c] = remote(
            full.at[0, c, count - 1], halo.at[c, 0], {"wide": lax.rem(me + 1, n_wide)}
        )
        leftward[c] = remote(
            full.at[0, c, 0], halo.at[c, 1], {"wide": lax.rem(me + n_wide - 1, n_wide)}
        )

    def need(index):
        if index not in loaded:
            loaded.add(index)
            loads[index].wait()

    def joined(product):
        real = product[:rows, :LANES] - product[rows:, LANES:]
        imag = product[rows:, :LANES] + product[:rows, LANES:]
        return real, imag

    def dot(left, right):
        return jnp.dot(left, right, preferred_element_type=jnp.float32)

    def begin(c):
        if c > 0:
            route[c - 1, 0].wait_send()
        route[c, 0].start()

    def pick(c, i):
        route[c, i].wait_recv()
        last = i == bits - 1

        @pl.loop(0, count)
        def _(j):
            held = x_ref[c, j] if i == 0 else xs[i - 1, c, j]
            value = jnp.where(bits_ref[i, j] != 0, rbuf[i, c, j], held)
            if last:
                full[0, c, j, own, :] = value
            else:
                xs[i, c, j] = value

        if last:
            narrow[c, 0].start()
            if local_bits == 0:
                wide[c, 0].start()
        else:
            route[c, i + 1].start()

    def pass_on(c, l):
        wide[c, l].wait_recv()
        forward[c, l].start()

    def level(c, l):
        need(l)
        narrow[c, l].wait_recv()
        if l == 0:
            @pl.when(me < n_wide - 1)
            def _():
                rightward[c].start()

            @pl.when(me > 0)
            def _():
                leftward[c].start()

        if l >= local_bits:
            forward[c, l].wait_recv()

        @pl.loop(0, count)
        def _(b):
            mine = dot(fac[l, b, 0], full[l, c, b])
            if l < local_bits:
                other = full[l, c, flipped(b, 1 << l)]
            else:
                other = part[l - local_bits, c, b]
            product = mine + keep_ref[l, b] * dot(fac[l, b, 1], other)
            real, imag = joined(product)
            if l < LEVELS - 1:
                full[l + 1, c, b, own, :LANES] = real.astype(jnp.bfloat16)
                full[l + 1, c, b, own, LANES:] = imag.astype(jnp.bfloat16)
            else:
                at = slice(c * LANES, (c + 1) * LANES)
                out_ref[b, 0, :, at] = out_ref[b, 0, :, at] + real
                out_ref[b, 1, :, at] = out_ref[b, 1, :, at] + imag

        if l < LEVELS - 1:
            if l + 1 >= local_bits:
                wide[c, l + 1].start()
            narrow[c, l + 1].start()

    def nearby(c):
        need(LEVELS)
        at = slice(c * LANES, (c + 1) * LANES)

        @pl.when(me > 0)
        def _():
            rightward[c].wait_recv()

        @pl.when(me == 0)
        def _():
            halo[c, 0] = jnp.zeros_like(halo[c, 0])

        @pl.when(me < n_wide - 1)
        def _():
            leftward[c].wait_recv()

        @pl.when(me == n_wide - 1)
        def _():
            halo[c, 1] = jnp.zeros_like(halo[c, 1])

        def put(b, left, right):
            product = dot(nea[b, 0], left) + dot(nea[b, 1], full[0, c, b]) + dot(nea[b, 2], right)
            real, imag = joined(product)
            out_ref[b, 0, :, at] = real
            out_ref[b, 1, :, at] = imag

        put(0, halo[c, 0], full[0, c, 1])

        @pl.loop(1, count - 1)
        def _(b):
            put(b, full[0, c, b - 1], full[0, c, b + 1])

        put(count - 1, full[0, c, count - 2], halo[c, 1])

    hop = 10.0
    steps = []
    for c in range(chunks):
        now = 2 * hop * c
        steps.append((now, functools.partial(begin, c)))
        for i, k in enumerate(order):
            now += 2 * hop if i == 0 else hop
            steps.append((now, functools.partial(pick, c, i)))
        for l in range(LEVELS):
            now += 2.0
            if l >= local_bits:
                now += hop if l < LEVELS - 1 else 2 * hop
                steps.append((now, functools.partial(pass_on, c, l)))
                now += 2.0
            steps.append((now, functools.partial(level, c, l)))
            if l == local_bits:
                steps.append((now + 0.5, functools.partial(nearby, c)))
    for _, step in sorted(steps, key=lambda item: item[0]):
        step()

    for c in range(chunks):
        for i in range(bits):
            if not (i == 0 and c < chunks - 1):
                route[c, i].wait_send()
        for l in range(LEVELS):
            narrow[c, l].wait_send()
            if l >= local_bits:
                wide[c, l].wait_send()
                forward[c, l].wait_send()

    @pl.when(me < n_wide - 1)
    def _():
        for c in range(chunks):
            rightward[c].wait_send()

    @pl.when(me > 0)
    def _():
        for c in range(chunks):
            leftward[c].wait_send()


def per_device(density, block_order, pattern, factors, near):
    count, _, rows, columns = density.shape
    n_wide = lax.axis_size("wide")
    bits = n_wide.bit_length() - 1
    chunks = columns // LANES
    exchanged = LEVELS - (count.bit_length() - 1)
    wide_at = lax.axis_index("wide")
    wanted = lax.dynamic_slice_in_dim(block_order, wide_at * count, count)
    masks = (wanted // count) ^ wide_at
    taken = jnp.take(density, wanted % count, axis=0)
    x = taken.reshape(count, 2, rows, chunks, LANES).transpose(3, 0, 2, 1, 4)
    x = x.reshape(chunks, count, rows, 2 * LANES)
    swap = jnp.stack([(masks >> k) & 1 for k in range(bits)[::-1]]).astype(jnp.int32)
    keep = lax.dynamic_slice_in_dim(pattern, wide_at * count, count, 1).astype(jnp.float32)
    size = factors.shape[-1]
    factors = factors.reshape(LEVELS, count, 2, 2 * rows, size)
    near = near.reshape(count, 3, 2 * rows, size)
    copies = chunks * (bits + LEVELS + 2 * exchanged + 2)
    bf16 = jnp.bfloat16
    return pl.pallas_call(
        functools.partial(kernel, n_wide),
        out_shape=jax.ShapeDtypeStruct((count, 2, rows, columns), jnp.float32),
        in_specs=[
            pl.BlockSpec(memory_space=pltpu.VMEM),
            pl.BlockSpec(memory_space=pltpu.SMEM),
            pl.BlockSpec(memory_space=pltpu.SMEM),
            pl.BlockSpec(memory_space=pl.ANY),
            pl.BlockSpec(memory_space=pl.ANY),
        ],
        out_specs=pl.BlockSpec(memory_space=pltpu.VMEM),
        scratch_shapes=[
            pltpu.VMEM(factors.shape, bf16),
            pltpu.VMEM(near.shape, bf16),
            pltpu.VMEM((bits,) + x.shape, bf16),
            pltpu.VMEM((max(bits - 1, 1),) + x.shape, bf16),
            pltpu.VMEM((LEVELS, chunks, count, size, 2 * LANES), bf16),
            pltpu.VMEM((exchanged, chunks, count, size, 2 * LANES), bf16),
            pltpu.VMEM((chunks, 2, size, 2 * LANES), bf16),
            pltpu.SemaphoreType.DMA((LEVELS + 1,)),
            pltpu.SemaphoreType.DMA((copies,)),
            pltpu.SemaphoreType.DMA((copies,)),
        ],
        compiler_params=pltpu.CompilerParams(
            collective_id=0, has_side_effects=True, vmem_limit_bytes=62 * 1024 * 1024
        ),
        cost_estimate=pl.CostEstimate(
            flops=2 * 4 * count * (2 * LEVELS + 3) * rows * size * columns,
            bytes_accessed=2 * (factors.size + near.size + x.size) + 4 * x.size,
            transcendentals=0,
        ),
    )(x, swap, keep, factors, near)


def solution(mesh):
    return jax.shard_map(
        per_device,
        mesh=mesh,
        in_specs=(
            P(("groups", "wide"), None, "narrow", None),
            P("groups"),
            P(None, "groups"),
            P(None, ("groups", "wide"), None, None, "narrow", None),
            P(("groups", "wide"), None, None, "narrow", None),
        ),
        out_specs=P(("groups", "wide"), None, "narrow", None),
        check_vma=False,
    )
```

time: 644 us -> 234 us (0.36); the launches traced: 632 us -> 234 us
  waiting for transfers between devices: 479 us -> 0 us
  Pallas kernels: 0 us -> 216 us
  local copies, waits for them, and re-layouts: 66.6 us -> 13.6 us
  matrix products: 48.7 us -> 0 us
  between operations: 14.3 us -> 0.03 us
  starting transfers between devices: 12.2 us -> 0 us
    ppermute x5 -> x0, waiting for transfers between devices: 257 us -> none  [the longest x3 247 us: swapped(): return lax.ppermute(block, axis, route)]
    all_gather x7 -> x0, waiting for transfers between devices: 222 us -> none  [the longest x1 180 us: per_device(): gathered = lax.all_gather(density, 'wide', axis=0, tiled=True)]
    pallas_call x0 -> x1, Pallas kernels: none -> 216 us  [per_device(): pl.pallas_call(functools.partial(kernel, n_wide), out_shape=jax.ShapeDtyp...]
    dot_general x60 -> x0, matrix products: 48.7 us -> none  [the longest x15 13.4 us: complex_apply(): jnp.einsum('boi,bir->bor', matrix[:, 0], vector[:, 0], preferred_element_...]
    squeeze x10 -> x0, local copies, waits for them, and re-layouts: 19.5 us -> none  [the longest x3 9.71 us: per_device(): factors[level_idx][:, 0]]
    unnamed x61 -> x3, local copies, waits for them, and re-layouts: 17.6 us -> 3.86 us
    ppermute x5 -> x0, starting transfers between devices: 11.6 us -> none  [the longest x3 6.79 us: swapped(): return lax.ppermute(block, axis, route)]
    slice x3 -> x0, local copies, waits for them, and re-layouts: 10.9 us -> none  [the longest x1 8.59 us: per_device(): factors[level_idx][:, 0]]
  transfers between devices with their start and end apart: 12 -> 0, of which waited for: 9 -> 0; matrix products, arithmetic and copies ran while one was open for 8% -> 0% of each run, Pallas kernels for 0% -> 0%
where the time goes in v1:
time: 234 us
  Pallas kernels  216 us (92%)
  local copies, waits for them, and re-layouts  13.6 us (6%)
  other arithmetic  4.17 us (2%)
    pallas_call x1, Pallas kernels, per_device(): pl.pallas_call(functools.partial(kernel, n_wide), out_shape=jax.ShapeDtyp...  216 us

profile of v1, /device:TPU:1, one launch (start us, length us, event | category | flops | bytes accessed | tf_op | source)
XLA Modules:
  0.0 233.7 jit_solution(13681026250867160075)
XLA Ops:
  0.0 0.0 copy-start
  0.0 0.9 and_bitcast_fusion.2
  0.9 0.6 pad_add_fusion.bits_ref
  1.5 1.4 dynamic-slice_convert_fusion.keep_ref
  2.8 0.0 copy-done
  2.8 1.9 gather_fusion
  4.7 1.9 copy.8
  6.6 1.4 select_bitcast_fusion
  8.0 3.6 %copy.9 = bf16[3,8,128,2,128]{4,3,2,1,0:T(2,128)(2,1)S(1)} copy(bf16[3,8,128,2,128]{2,4,0,3,1:T(8,128)(2,1)} %select_bitcast_fusion) | data formatting | bytes 3145728 | tf_op jit(solution)/shard_map/transpose | solution.py:243
  11.6 2.3 reshape.16.x_ref
  13.9 215.9 %shard_map.55 = f32[8,2,128,384]{3,2,1,0:T(8,128)} custom-call(bf16[3,8,128,256]{3,2,1,0:T(8,128)(2,1)} %reshape.16.x_ref, s32[3,8]{1,0:T(4,128)} %pad_add_fusion.bits_ref, f32[6,8]{1,0:T(8,128)} %dynamic-slice_convert_fusion.keep_ref, bf16[6,8,2,256,256]{4,3,2,1,0:T(8,128)(2,1)} %bitcast.12, bf16[8,3,256,256]{3,2,1,0:T(8,128)(2,1)} %bitcast.13), custom_call_target="tpu_custom_call" | custom-call | flops 12079595520 | bytes 20447232 | tf_op jit(solution)/shard_map/pallas_call | solution.py:252
  229.8 3.9 %copy.11 = f32[8,2,128,384]{3,2,1,0:T(8,128)} copy(f32[8,2,128,384]{3,2,1,0:T(8,128)} %shard_map.55) | data formatting | bytes 6291456
  (3 shorter events, 0.0 us)
Async XLA Ops:
  0.0 2.8 %copy-start = (bf16[8,2,128,384]{3,2,1,0:T(8,128)(2,1)S(1)}, bf16[8,2,128,384]{3,2,1,0:T(8,128)(2,1)}, u32[]{:S(2)}) copy-start(bf16[8,2,128,384]{3,2,1,0:T(8,128)(2,1)} %param.5) | copy-start | bytes 4718596

commit v2 on v1

--- a/solution.py
+++ b/solution.py
@@ -9,6 +9,8 @@
 
 LEVELS = 6
 LANES = 128
+GROUPS = 2
+SERIAL = False
 MESH = pl.DeviceIdType.MESH
 
 
@@ -16,11 +18,17 @@
     return index + distance * (1 - 2 * lax.rem(lax.div(index, distance), 2))
 
 
+def flipped_bits(index, other):
+    return index ^ other
+
+
 def kernel(
-    n_wide, x_ref, bits_ref, keep_ref, factors_hbm, near_hbm, out_ref,
+    n_wide, density_ref, order_ref, pattern_ref, factors_hbm, near_hbm, out_ref,
     fac, nea, rbuf, xs, full, part, halo, load_sem, send_sem, recv_sem,
 ):
-    chunks, count, rows, lanes = x_ref.shape
+    chunks, count, rows, lanes = xs.shape[1:]
+    pieces = [pl.ds(g * (count // GROUPS), count // GROUPS) for g in range(GROUPS)]
+    spans = [(g * (count // GROUPS), (g + 1) * (count // GROUPS)) for g in range(GROUPS)]
     bits = n_wide.bit_length() - 1
     local_bits = count.bit_length() - 1
     me = lax.axis_index("wide")
@@ -39,6 +47,18 @@
             barrier, inc=1, device_id={"wide": lax.rem(me + other, n_wide)}, device_id_type=MESH
         )
     pl.semaphore_signal(barrier, inc=1, device_id={"narrow": 1 - core}, device_id_type=MESH)
+
+    def take(c):
+        at = slice(c * LANES, (c + 1) * LANES)
+
+        @pl.loop(0, count)
+        def _(j):
+            slot = lax.rem(order_ref[me * count + j], count)
+            xs[0, c, j, :, :LANES] = density_ref[slot, 0, :, at]
+            xs[0, c, j, :, LANES:] = density_ref[slot, 1, :, at]
+
+    for c in range(chunks):
+        take(c)
     pl.semaphore_wait(barrier, n_wide)
 
     made = []
@@ -58,16 +78,19 @@
     route, narrow, wide, forward, rightward, leftward = {}, {}, {}, {}, {}, {}
     for c in range(chunks):
         for i, k in enumerate(order):
-            src = x_ref.at[c] if i == 0 else xs.at[i - 1, c]
-            route[c, i] = remote(src, rbuf.at[i, c], {"wide": flipped(me, 1 << k)})
+            for g, piece in enumerate(pieces):
+                route[c, g, i] = remote(
+                    xs.at[i, c, piece], rbuf.at[i, c, piece], {"wide": flipped(me, 1 << k)}
+                )
         for l in range(LEVELS):
-            half = full.at[l, c, :, own, :]
-            narrow[c, l] = remote(half, half, sibling)
-            if l >= local_bits:
-                w = l - local_bits
-                held = part.at[w, c, :, own, :]
-                wide[c, l] = remote(half, held, {"wide": flipped(me, 1 << w)})
-                forward[c, l] = remote(held, held, sibling)
+            for g, piece in enumerate(pieces):
+                half = full.at[l, c, piece, own, :]
+                narrow[c, g, l] = remote(half, half, sibling)
+                if l >= local_bits:
+                    w = l - local_bits
+                    held = part.at[w, c, piece, own, :]
+                    wide[c, g, l] = remote(half, held, {"wide": flipped(me, 1 << w)})
+                    forward[c, g, l] = remote(held, held, sibling)
     for c in range(chunks):
         rightward[c] = remote(
             full.at[0, c, count - 1], halo.at[c, 0], {"wide": lax.rem(me + 1, n_wide)}
@@ -89,58 +112,60 @@
     def dot(left, right):
         return jnp.dot(left, right, preferred_element_type=jnp.float32)
 
-    def begin(c):
-        if c > 0:
-            route[c - 1, 0].wait_send()
-        route[c, 0].start()
-
-    def pick(c, i):
-        route[c, i].wait_recv()
+    sent = set()
+
+    def begin(c, g):
+        before = (c, g - 1, 0) if g else (c - 1, GROUPS - 1, 0)
+        if SERIAL and c + g > 0:
+            route[before].wait_send()
+            sent.add(before)
+        route[c, g, 0].start()
+
+    def pick(c, g, i):
+        route[c, g, i].wait_recv()
         last = i == bits - 1
 
-        @pl.loop(0, count)
+        @pl.loop(*spans[g])
         def _(j):
-            held = x_ref[c, j] if i == 0 else xs[i - 1, c, j]
-            value = jnp.where(bits_ref[i, j] != 0, rbuf[i, c, j], held)
+            mask = flipped_bits(lax.div(order_ref[me * count + j], count), me)
+            bit = lax.rem(lax.div(mask, 1 << order[i]), 2)
+            value = jnp.where(bit != 0, rbuf[i, c, j], xs[i, c, j])
             if last:
                 full[0, c, j, own, :] = value
             else:
-                xs[i, c, j] = value
+                xs[i + 1, c, j] = value
 
         if last:
-            narrow[c, 0].start()
-            if local_bits == 0:
-                wide[c, 0].start()
+            narrow[c, g, 0].start()
         else:
-            route[c, i + 1].start()
-
-    def pass_on(c, l):
-        wide[c, l].wait_recv()
-        forward[c, l].start()
-
-    def level(c, l):
-        need(l)
-        narrow[c, l].wait_recv()
-        if l == 0:
-            @pl.when(me < n_wide - 1)
-            def _():
-                rightward[c].start()
-
-            @pl.when(me > 0)
-            def _():
-                leftward[c].start()
-
-        if l >= local_bits:
-            forward[c, l].wait_recv()
-
-        @pl.loop(0, count)
+            route[c, g, i + 1].start()
+
+    def pass_on(c, g, l):
+        wide[c, g, l].wait_recv()
+        forward[c, g, l].start()
+
+    def edges(c):
+        for g in range(GROUPS):
+            narrow[c, g, 0].wait_recv()
+
+        @pl.when(me < n_wide - 1)
+        def _():
+            rightward[c].start()
+
+        @pl.when(me > 0)
+        def _():
+            leftward[c].start()
+
+    def apply(c, g, l):
+        @pl.loop(*spans[g])
         def _(b):
             mine = dot(fac[l, b, 0], full[l, c, b])
             if l < local_bits:
                 other = full[l, c, flipped(b, 1 << l)]
             else:
                 other = part[l - local_bits, c, b]
-            product = mine + keep_ref[l, b] * dot(fac[l, b, 1], other)
+            keep = pattern_ref[l, me * count + b].astype(jnp.float32)
+            product = mine + keep * dot(fac[l, b, 1], other)
             real, imag = joined(product)
             if l < LEVELS - 1:
                 full[l + 1, c, b, own, :LANES] = real.astype(jnp.bfloat16)
@@ -152,8 +177,24 @@
 
         if l < LEVELS - 1:
             if l + 1 >= local_bits:
-                wide[c, l + 1].start()
-            narrow[c, l + 1].start()
+                wide[c, g, l + 1].start()
+            narrow[c, g, l + 1].start()
+
+    def level_local(c, l):
+        need(l)
+        if l == 0:
+            edges(c)
+        else:
+            for g in range(GROUPS):
+                narrow[c, g, l].wait_recv()
+        for g in range(GROUPS):
+            apply(c, g, l)
+
+    def level_wide(c, g, l):
+        need(l)
+        narrow[c, g, l].wait_recv()
+        forward[c, g, l].wait_recv()
+        apply(c, g, l)
 
     def nearby(c):
         need(LEVELS)
@@ -189,35 +230,47 @@
 
         put(count - 1, full[0, c, count - 2], halo[c, 1])
 
-    hop = 10.0
+    hop = 9.0 / GROUPS
+    free = {}
+
+    def travel(bit, ready):
+        start = max(ready, free.get(bit, 0.0))
+        free[bit] = start + hop * (2.0 if bit == bits - 1 else 1.0)
+        return start, free[bit]
+
     steps = []
-    for c in range(chunks):
-        now = 2 * hop * c
-        steps.append((now, functools.partial(begin, c)))
-        for i, k in enumerate(order):
-            now += 2 * hop if i == 0 else hop
-            steps.append((now, functools.partial(pick, c, i)))
-        for l in range(LEVELS):
+    ready = {}
+    for c in range(chunks):
+        for g in range(GROUPS):
+            now = 0.0
+            for i, k in enumerate(order):
+                start, now = travel(k, now)
+                if i == 0:
+                    steps.append((start, functools.partial(begin, c, g)))
+                steps.append((now, functools.partial(pick, c, g, i)))
+            ready[c, g] = now
+    for c in range(chunks):
+        now = max(ready[c, g] for g in range(GROUPS))
+        for l in range(local_bits):
             now += 2.0
-            if l >= local_bits:
-                now += hop if l < LEVELS - 1 else 2 * hop
-                steps.append((now, functools.partial(pass_on, c, l)))
-                now += 2.0
-            steps.append((now, functools.partial(level, c, l)))
-            if l == local_bits:
-                steps.append((now + 0.5, functools.partial(nearby, c)))
+            steps.append((now, functools.partial(level_local, c, l)))
+        steps.append((now + 0.5, functools.partial(nearby, c)))
+        for g in range(GROUPS):
+            then = now
+            for l in range(local_bits, LEVELS):
+                _, then = travel(l - local_bits, then)
+                steps.append((then, functools.partial(pass_on, c, g, l)))
+                then += 2.0
+                steps.append((then, functools.partial(level_wide, c, g, l)))
     for _, step in sorted(steps, key=lambda item: item[0]):
         step()
 
-    for c in range(chunks):
-        for i in range(bits):
-            if not (i == 0 and c < chunks - 1):
-                route[c, i].wait_send()
-        for l in range(LEVELS):
-            narrow[c, l].wait_send()
-            if l >= local_bits:
-                wide[c, l].wait_send()
-                forward[c, l].wait_send()
+    for key, copy in route.items():
+        if key not in sent:
+            copy.wait_send()
+    for copies in (narrow, wide, forward):
+        for copy in copies.values():
+            copy.wait_send()
 
     @pl.when(me < n_wide - 1)
     def _():
@@ -236,18 +289,11 @@
     bits = n_wide.bit_length() - 1
     chunks = columns // LANES
     exchanged = LEVELS - (count.bit_length() - 1)
-    wide_at = lax.axis_index("wide")
-    wanted = lax.dynamic_slice_in_dim(block_order, wide_at * count, count)
-    masks = (wanted // count) ^ wide_at
-    taken = jnp.take(density, wanted % count, axis=0)
-    x = taken.reshape(count, 2, rows, chunks, LANES).transpose(3, 0, 2, 1, 4)
-    x = x.reshape(chunks, count, rows, 2 * LANES)
-    swap = jnp.stack([(masks >> k) & 1 for k in range(bits)[::-1]]).astype(jnp.int32)
-    keep = lax.dynamic_slice_in_dim(pattern, wide_at * count, count, 1).astype(jnp.float32)
+    shape = (chunks, count, rows, 2 * LANES)
     size = factors.shape[-1]
     factors = factors.reshape(LEVELS, count, 2, 2 * rows, size)
     near = near.reshape(count, 3, 2 * rows, size)
-    copies = chunks * (bits + LEVELS + 2 * exchanged + 2)
+    copies = chunks * (GROUPS * (bits + LEVELS + 2 * exchanged) + 2)
     bf16 = jnp.bfloat16
     return pl.pallas_call(
         functools.partial(kernel, n_wide),
@@ -263,8 +309,8 @@
         scratch_shapes=[
             pltpu.VMEM(factors.shape, bf16),
             pltpu.VMEM(near.shape, bf16),
-            pltpu.VMEM((bits,) + x.shape, bf16),
-            pltpu.VMEM((max(bits - 1, 1),) + x.shape, bf16),
+            pltpu.VMEM((bits,) + shape, bf16),
+            pltpu.VMEM((bits,) + shape, bf16),
             pltpu.VMEM((LEVELS, chunks, count, size, 2 * LANES), bf16),
             pltpu.VMEM((exchanged, chunks, count, size, 2 * LANES), bf16),
             pltpu.VMEM((chunks, 2, size, 2 * LANES), bf16),
@@ -277,10 +323,10 @@
         ),
         cost_estimate=pl.CostEstimate(
             flops=2 * 4 * count * (2 * LEVELS + 3) * rows * size * columns,
-            bytes_accessed=2 * (factors.size + near.size + x.size) + 4 * x.size,
+            bytes_accessed=2 * (factors.size + near.size + density.size) + 4 * density.size,
             transcendentals=0,
         ),
-    )(x, swap, keep, factors, near)
+    )(density, block_order, pattern, factors, near)
 
 
 def solution(mesh):

time: 234 us -> 222 us (0.949)
  local copies, waits for them, and re-layouts: 13.6 us -> 3.86 us
  other arithmetic: 4.17 us -> 0 us
    gather x2 -> x0, local copies, waits for them, and re-layouts: 3.82 us -> none  [per_device(): taken = jnp.take(density, wanted % count, axis=0)]
    transpose x1 -> x0, local copies, waits for them, and re-layouts: 3.62 us -> none  [per_device(): x = taken.reshape(count, 2, rows, chunks, LANES).transpose(3, 0, 2, 1, 4)]
where the time goes in v2:
time: 222 us
  Pallas kernels  218 us (98%)
  local copies, waits for them, and re-layouts  3.86 us (2%)
    pallas_call x1, Pallas kernels, per_device(): pl.pallas_call(functools.partial(kernel, n_wide), out_shape=jax.ShapeDtyp...  218 us

profile of v2, /device:TPU:1, one launch (start us, length us, event | category | flops | bytes accessed | tf_op | source)
XLA Modules:
  0.0 222.0 jit_solution(444373783647343429)
XLA Ops:
  0.0 218.1 %shard_map.55 = f32[8,2,128,384]{3,2,1,0:T(8,128)} custom-call(bf16[8,2,128,384]{3,2,1,0:T(8,128)(2,1)} %density_ref.1, s32[64]{0:T(128)} %order_ref.1, s32[6,64]{1,0:T(8,128)} %pattern_ref.1, bf16[6,8,2,256,256]{4,3,2,1,0:T(8,128)(2,1)} %bitcast.2, bf16[8,3,256,256]{3,2,1,0:T(8,128)(2,1)} %bitcast.3), custom_call_target="tpu_custom_call" | custom-call | flops 12079595520 | bytes 20447232 | tf_op jit(solution)/shard_map/pallas_call | solution.py:298
  218.1 3.9 %copy.7 = f32[8,2,128,384]{3,2,1,0:T(8,128)} copy(f32[8,2,128,384]{3,2,1,0:T(8,128)} %shard_map.55) | data formatting | bytes 6291456
